TPU v7x, 256 devices: a whole 4x4x8 slice. The times are simulated.
256 devices in a mesh: dp: 8 (over z_hi, core), seq: 32 (over y, z_lo, x).
Axes of the slice: x: 4, y: 4, z: 8 (z_hi: 4, z_lo: 2; z = z_hi * 2 + z_lo), core: 2. Of those that a mesh axis runs over, the one named last changes fastest.
Arguments:
- frames: bfloat16 [8, 4096, 1536], P('dp', 'seq'), may hold values from -6 to 6
- w_qkv: bfloat16 [1536, 2304], P('seq'), may hold values from -0.26791294 to 0.26791294
- w_out: bfloat16 [768, 1536], P('seq'), may hold values from -0.21875 to 0.21875
- norm_gains: float32 [2, 1536], replicated, may hold values from 0.1 to 1.9
- conv_kernel: float32 [31, 1536], replicated, may hold values from -1 to 1
- conv_bias: float32 [1536], replicated, may hold values from -3 to 3
- out_grad: bfloat16 [8, 4096, 1536], P('dp', 'seq'), may hold values from -6 to 6
Outputs:
- block_out: bfloat16 [8, 4096, 1536], P('dp', 'seq')
- grad_input: bfloat16 [8, 4096, 1536], P('dp', 'seq')
- grad_qkv: bfloat16 [1536, 2304], P('seq')
- grad_out: bfloat16 [768, 1536], P('seq')
- grad_norms: float32 [2, 1536], replicated
- grad_kernel: float32 [31, 1536], replicated
- grad_bias: float32 [1536], replicated
All inputs are finite; a program needn't handle non-finite values.
Results may differ from a plain program's by a relative error of at most 0.035.
Values may be sent and summed in bfloat16 or wider, within the bound.
A program may use at most 64 MiB of HBM per device.

v0:
```python
import math

import jax
import jax.numpy as jnp
from jax import lax
from jax.sharding import PartitionSpec as P

H = 12


EPS = 1e-05


def padded(array, sides, width):
    for axis, dim in sides:
        devices, length = (lax.axis_size(axis), array.shape[dim])
        up = [(i, (i + 1) % devices) for i in range(devices - 1)]
        down = [(j, i) for i, j in up]
        last = lax.slice_in_dim(array, length - width, length, axis=dim)
        initial = lax.slice_in_dim(array, 0, width, axis=dim)
        before = lax.ppermute(last, axis, up)
        after = lax.ppermute(initial, axis, down)
        array = jnp.concatenate([before, array, after], axis=dim)
    return array


def layer_norm(values, gain):
    center = values - jnp.mean(values, axis=-1, keepdims=True)
    spread = jnp.mean(center * center, axis=-1, keepdims=True)
    inverse = lax.rsqrt(spread + EPS)
    normed = center * inverse
    return (normed * gain, normed, inverse)


def norm_back(grad, normed, inverse, gain):
    scaled = grad * gain
    inner = (
        scaled
        - jnp.mean(scaled, axis=-1, keepdims=True)
        - normed * jnp.mean(scaled * normed, axis=-1, keepdims=True)
    )
    return (inverse * inner, jnp.sum(grad * normed, axis=0))


def head_forward(query, keys, values):
    factor = query.shape[-1] ** (-0.5)
    scores = (
        lax.dot_general(query, keys, (((1,), (1,)), ((), ())), preferred_element_type=jnp.float32)
        * factor
    )
    top = jnp.max(scores, axis=-1, keepdims=True)
    expo = jnp.exp(scores - top)
    total = jnp.sum(expo, axis=-1, keepdims=True)
    probs = (expo / total).astype(jnp.bfloat16)
    attended = jnp.dot(probs, values, preferred_element_type=jnp.float32).astype(jnp.bfloat16)
    return (attended, top[:, 0] + jnp.log(total[:, 0]))


def head_backward(query, keys, values, attended, log_total, grad_attended):
    factor = query.shape[-1] ** (-0.5)
    scores = (
        lax.dot_general(query, keys, (((1,), (1,)), ((), ())), preferred_element_type=jnp.float32)
        * factor
    )
    probs = jnp.exp(scores - log_total[:, None])
    value_grads = lax.dot_general(
        probs.astype(jnp.bfloat16),
        grad_attended,
        (((0,), (0,)), ((), ())),
        preferred_element_type=jnp.float32,
    )
    prob_grads = lax.dot_general(
        grad_attended, values, (((1,), (1,)), ((), ())), preferred_element_type=jnp.float32
    )
    delta = jnp.sum(
        grad_attended.astype(jnp.float32) * attended.astype(jnp.float32), axis=-1, keepdims=True
    )
    score_grads = (probs * (prob_grads - delta) * factor).astype(jnp.bfloat16)
    query_grads = jnp.dot(score_grads, keys, preferred_element_type=jnp.float32)
    key_grads = lax.dot_general(
        score_grads, query, (((0,), (0,)), ((), ())), preferred_element_type=jnp.float32
    )
    return (query_grads, key_grads, value_grads)


def depthwise(wide, kernel, length):
    total = jnp.zeros((length, wide.shape[1]), jnp.float32)
    for tap in range(kernel.shape[0]):
        total = total + wide[tap : tap + length] * kernel[tap]
    return total


def to_groups(values, count, groups, quarters):
    rows, span = values.shape
    width = span // groups
    return (
        values.reshape(quarters, rows // quarters, groups, width)
        .transpose(2, 0, 1, 3)
        .reshape(count, rows // quarters, width)
    )


def from_groups(values, groups, quarters):
    count, share, width = values.shape
    return (
        values.reshape(groups, quarters, share, width)
        .transpose(1, 2, 0, 3)
        .reshape(quarters * share, groups * width)
    )


def spread_keys(keys, values, groups, quarters):
    rows = keys.shape[0]
    width = keys.shape[1] // groups
    both = jnp.concatenate(
        [keys.reshape(rows, groups, width), values.reshape(rows, groups, width)], axis=2
    ).transpose(1, 0, 2)
    return jnp.broadcast_to(both[:, None], (groups, quarters, rows, 2 * width)).reshape(
        groups * quarters, rows, 2 * width
    )


def split_heads(block, per_group):
    return block.reshape(block.shape[0], per_group, -1).transpose(1, 0, 2)


def join_heads(block):
    return block.transpose(1, 0, 2).reshape(block.shape[1], -1)


def local(frames, w_qkv, w_out, norm_gains, conv_kernel, conv_bias, out_grad):
    count = lax.axis_size("seq")
    groups = math.gcd(H, count)
    quarters = count // groups
    per_group = H // groups
    inputs = frames[0].astype(jnp.float32)
    rows = inputs.shape[0]
    w_full, out_full = (
        lax.all_gather(w_qkv, "seq", axis=0, tiled=True),
        lax.all_gather(w_out, "seq", axis=0, tiled=True),
    )
    width_all = out_full.shape[0]
    width = width_all // groups
    shifted, normed1, inverse1 = layer_norm(inputs, norm_gains[0])
    hidden = shifted.astype(jnp.bfloat16)
    projected = jnp.dot(hidden, w_full, preferred_element_type=jnp.float32).astype(jnp.bfloat16)
    query_send = to_groups(projected[:, :width_all], count, groups, quarters)
    key_send = spread_keys(
        projected[:, width_all : 2 * width_all], projected[:, 2 * width_all :], groups, quarters
    )
    query_recv, key_recv = (
        lax.all_to_all(query_send, "seq", split_axis=0, concat_axis=0, tiled=True),
        lax.all_to_all(key_send, "seq", split_axis=0, concat_axis=0, tiled=True),
    )
    query_heads = split_heads(query_recv.reshape(-1, width), per_group)
    key_rows = key_recv.reshape(-1, 2 * width)
    key_heads = split_heads(key_rows[:, :width], per_group)
    value_heads = split_heads(key_rows[:, width:], per_group)
    attended_heads, log_total = lax.map(
        lambda item: head_forward(item[0], item[1], item[2]), (query_heads, key_heads, value_heads)
    )
    attended_home = lax.all_to_all(
        join_heads(attended_heads).reshape(count, rows // quarters, width),
        "seq",
        split_axis=0,
        concat_axis=0,
        tiled=True,
    )
    attended = from_groups(attended_home, groups, quarters)
    mixed = (inputs + jnp.dot(attended, out_full, preferred_element_type=jnp.float32)).astype(
        jnp.bfloat16
    )
    mixed32 = mixed.astype(jnp.float32)
    shifted2, normed2, inverse2 = layer_norm(mixed32, norm_gains[1])
    conv_in = shifted2.astype(jnp.bfloat16)
    taps = conv_kernel.shape[0]
    half = (taps - 1) // 2
    conv_wide = padded(conv_in, (("seq", 0),), half).astype(jnp.float32)
    preact = depthwise(conv_wide, conv_kernel, rows) + conv_bias
    sigma = jax.nn.sigmoid(preact)
    output = (mixed32 + preact * sigma).astype(jnp.bfloat16)
    upstream = out_grad[0].astype(jnp.float32)
    grad_pre = (upstream * sigma * (1.0 + preact * (1.0 - sigma))).astype(jnp.bfloat16)
    grad_pre_wide = padded(grad_pre, (("seq", 0),), half).astype(jnp.float32)
    grad_conv = depthwise(grad_pre_wide, conv_kernel[::-1], rows)
    grad_pre_float = grad_pre.astype(jnp.float32)
    kernel_grad = jnp.stack(
        [jnp.sum(grad_pre_float * conv_wide[tap : tap + rows], axis=0) for tap in range(taps)]
    )
    bias_grad = jnp.sum(grad_pre_float, axis=0)
    mixed_norm_grad, gain2_grad = norm_back(grad_conv, normed2, inverse2, norm_gains[1])
    grad_mixed = (upstream + mixed_norm_grad).astype(jnp.bfloat16)
    grad_attended = lax.dot_general(
        grad_mixed, out_full, (((1,), (1,)), ((), ())), preferred_element_type=jnp.float32
    ).astype(jnp.bfloat16)
    grad_recv = lax.all_to_all(
        to_groups(grad_attended, count, groups, quarters),
        "seq",
        split_axis=0,
        concat_axis=0,
        tiled=True,
    )
    grad_heads = split_heads(grad_recv.reshape(-1, width), per_group)
    query_grads, key_grads, value_grads = lax.map(
        lambda item: head_backward(item[0], item[1], item[2], item[3], item[4], item[5]),
        (query_heads, key_heads, value_heads, attended_heads, log_total, grad_heads),
    )
    query_send_back = (
        join_heads(query_grads).reshape(count, rows // quarters, width).astype(jnp.bfloat16)
    )
    pair_send = (
        jnp.concatenate([join_heads(key_grads), join_heads(value_grads)], axis=1)
        .reshape(count, rows, 2 * width)
        .astype(jnp.bfloat16)
    )
    query_home, pair_home = (
        lax.all_to_all(query_send_back, "seq", split_axis=0, concat_axis=0, tiled=True),
        lax.all_to_all(pair_send, "seq", split_axis=0, concat_axis=0, tiled=True),
    )
    query_final = from_groups(query_home, groups, quarters)
    summed = jnp.sum(
        pair_home.astype(jnp.float32).reshape(groups, quarters, rows, 2 * width), axis=1
    )
    key_final = (
        summed[:, :, :width].transpose(1, 0, 2).reshape(rows, width_all).astype(jnp.bfloat16)
    )
    value_final = (
        summed[:, :, width:].transpose(1, 0, 2).reshape(rows, width_all).astype(jnp.bfloat16)
    )
    grad_proj = jnp.concatenate([query_final, key_final, value_final], axis=1)
    grad_hidden = lax.dot_general(
        grad_proj, w_full, (((1,), (1,)), ((), ())), preferred_element_type=jnp.float32
    )
    input_norm_grad, gain1_grad = norm_back(grad_hidden, normed1, inverse1, norm_gains[0])
    grad_input = (grad_mixed.astype(jnp.float32) + input_norm_grad).astype(jnp.bfloat16)
    proj_whole = lax.dot_general(
        hidden, grad_proj, (((0,), (0,)), ((), ())), preferred_element_type=jnp.float32
    )
    out_whole = lax.dot_general(
        attended, grad_mixed, (((0,), (0,)), ((), ())), preferred_element_type=jnp.float32
    )
    proj_sum, out_sum = (
        lax.psum_scatter(
            proj_whole.astype(jnp.bfloat16), "seq", scatter_dimension=0, tiled=True
        ).astype(jnp.float32),
        lax.psum_scatter(
            out_whole.astype(jnp.bfloat16), "seq", scatter_dimension=0, tiled=True
        ).astype(jnp.float32),
    )
    norms_local = jnp.stack([gain1_grad, gain2_grad])
    norms_sum, kernel_sum, bias_sum = lax.psum((norms_local, kernel_grad, bias_grad), ("dp", "seq"))
    proj_sum, out_sum = (
        lax.psum(proj_sum.astype(jnp.bfloat16), "dp").astype(jnp.float32),
        lax.psum(out_sum.astype(jnp.bfloat16), "dp").astype(jnp.float32),
    )
    return (
        output[None],
        grad_input[None],
        proj_sum.astype(jnp.bfloat16),
        out_sum.astype(jnp.bfloat16),
        norms_sum,
        kernel_sum,
        bias_sum,
    )


def solution(mesh):
    in_specs = (
        P("dp", "seq", None),
        P("seq", None),
        P("seq", None),
        P(),
        P(),
        P(),
        P("dp", "seq", None),
    )
    out_specs = (
        P("dp", "seq", None),
        P("dp", "seq", None),
        P("seq", None),
        P("seq", None),
        P(),
        P(),
        P(),
    )
    return jax.shard_map(local, mesh=mesh, in_specs=in_specs, out_specs=out_specs, check_vma=False)
```

profile of v0, /device:TPU:1, one launch (start us, length us, event | category | flops | bytes accessed | tf_op | source)
XLA Modules:
  0.0 1185.1 jit_solution(8754148829194041722)
XLA Ops:
  11.1 149.5 %all-gather.3.cloned.1.call-done = bf16[1536,2304]{1,0:T(8,128)(2,1)} async-done(((bf16[48,2304]{1,0:T(8,128)(2,1)}), bf16[1536,2304]{1,0:T(8,128)(2,1)}) %all-gather.3.cloned.1.call-update) | async-done | bytes 7077904 | tf_op jit(solution)/shard_map/all_gather | solution.py:139
  166.0 6.5 all-to-all-start
  172.8 7.6 all-to-all-done
  182.9 4.8 all-to-all-start.1
  188.7 24.2 %all-to-all-done.1 = bf16[32,128,384]{1,2,0:T(8,128)(2,1)} async-done(((bf16[32,128,384]{1,2,0:T(8,128)(2,1)}), bf16[32,128,384]{1,2,0:T(8,128)(2,1)}, u32[]{:S(2)}, u32[]{:S(2)}) %all-to-all-start.1) | async-done | bytes 3145760 | tf_op jit(solution)/shard_map/all_to_all | solution.py:153
  223.6 26.1 %while.26 = (s32[]{:T(128)}, bf16[3,512,64]{1,2,0:T(8,128)(2,1)S(1)}, f32[3,512]{1,0:T(4,128)}, bf16[3,512,64]{2,1,0:T(8,128)(2,1)S(1)}, bf16[3,4096,64]{2,1,0:T...) while((s32[]{:T(128)}, bf16[3,512,64]{1,2,0:T(8,128)(2,1)S(1)}, f32[3,512]{1,0:T(4,128)}, ...), condition=%wide.region_5.6_spmd, body=%wide.region_2.5_spmd.sunk | while | flops 555777536 | bytes 27482208 | solution.py:159
  251.1 5.6 all-to-all-start.2
  257.0 7.8 all-to-all-done.2
  265.3 95.2 %all-gather.5.cloned.1.call-done = bf16[768,1536]{1,0:T(8,128)(2,1)} async-done(((bf16[24,1536]{1,0:T(8,128)(2,1)}), bf16[768,1536]{1,0:T(8,128)(2,1)}) %all-gather.5.cloned.1.call-update) | async-done | bytes 2359312 | tf_op jit(solution)/shard_map/all_gather | solution.py:140
  369.9 6.5 fusion.94
  382.7 4.8 multiply_reduce_fusion.1
  391.1 7.3 all-to-all-start.3
  398.5 7.9 all-to-all-done.3
  408.5 44.5 %while.27 = (s32[]{:T(128)}, bf16[3,512,64]{1,2,0:T(8,128)(2,1)}, bf16[3,4096,64]{1,2,0:T(8,128)(2,1)}, bf16[3,4096,64]{1,2,0:T(8,128)(2,1)}, bf16[3,512,64]{2,1...) while((s32[]{:T(128)}, bf16[3,512,64]{1,2,0:T(8,128)(2,1)}, ...), condition=%wide.region_12.13_spmd, body=%wide.region_10.12_spmd.sunk | while | flops 1361182208 | bytes 70796584 | solution.py:204
  413.8 4.7 multiply_convert_fusion.3
  467.4 5.3 all-to-all-start.5
  475.7 21.8 %all-to-all-done.5 = bf16[32,128,384]{1,2,0:T(8,128)(2,1)} async-done(((bf16[32,128,384]{1,2,0:T(8,128)(2,1)}), bf16[32,128,384]{1,2,0:T(8,128)(2,1)}, u32[]{:S(2)}, u32[]{:S(2)}) %all-to-all-start.5) | async-done | bytes 3145760 | tf_op jit(solution)/shard_map/all_to_all | solution.py:218
  500.6 5.1 convolution_convert_fusion
  510.7 5.5 fusion.59
  516.2 107.6 %all-reduce = (f32[2,1536]{1,0:T(2,128)}, f32[1536]{0:T(1024)}) all-reduce(f32[2,1536]{1,0:T(2,128)S(1)} %pad_maximum_fusion.4, f32[1536]{0:T(1024)S(1)} %get-tuple-element.194), channel_id=1, replica_groups=mesh['dp'=8,'seq'=32] {'dp','seq'}, use_global_device_ids=true, to_apply=%region_22.23 | all-reduce | flops 4608 | bytes 36864 | tf_op jit(solution)/shard_map/psum | solution.py:251
  623.9 27.0 %reduce-scatter.5.cloned.1.call-done = bf16[24,1536]{1,0:T(8,128)(2,1)} async-done(((bf16[768,1536]{1,0:T(8,128)(2,1)}), bf16[24,1536]{1,0:T(8,128)(2,1)}) %reduce-scatter.5.cloned.1.call-update) | async-done | bytes 73744 | tf_op jit(solution)/shard_map/reduce_scatter | solution.py:246
  650.9 178.3 %reduce-scatter.3.cloned.1.call-done = bf16[48,2304]{1,0:T(8,128)(2,1)} async-done(((bf16[1536,2304]{1,0:T(8,128)(2,1)}), bf16[48,2304]{1,0:T(8,128)(2,1)}) %reduce-scatter.3.cloned.1.call-update) | async-done | bytes 221200 | tf_op jit(solution)/shard_map/reduce_scatter | solution.py:243
  830.4 269.2 %all-reduce.5.cloned.1.call-done = f32[31,1536]{1,0:T(8,128)} async-done(((f32[31,1536]{1,0:T(8,128)}), f32[31,1536]{1,0:T(8,128)}) %all-reduce.5.cloned.1.call-update) | async-done | bytes 190480 | tf_op jit(solution)/shard_map/psum | solution.py:251
  1099.6 73.6 %all-reduce.7.cloned.1.call-done = (bf16[48,2304]{1,0:T(8,128)(2,1)}, bf16[24,1536]{1,0:T(8,128)(2,1)}) async-done(((bf16[48,2304]{1,0:T(8,128)(2,1)}, bf16[24,1536]{1,0:T(8,128)(2,1)}), (bf16[48,2304]{1,0:T(8,128)(2,1)}, bf16[24,1536]{1,0:T(8,128)(2,1)})) %all-reduce.7.cloned.1.call-update) | async-done | bytes 294928 | tf_op jit(solution)/shard_map/psum | solution.py:253
  (264 shorter events, 143.4 us)
Async XLA Ops:
  7.2 153.4 %all-gather.3.cloned.1.call-start = ((), (), s32[]{:S(2)}) async-start(), calls=%async_computation.8 | async-start | bytes 7299072 | tf_op jit(solution)/shard_map/all_gather | solution.py:139
  8.7 151.9 %copy-start.8 = (f32[1536]{0:T(1024)}, f32[1536]{0:T(1024)S(1)}, u32[]{:S(2)}) copy-start(f32[1536]{0:T(1024)S(1)} %get-tuple-element.227) | copy-start | bytes 18436
  9.9 150.7 %copy-start.31 = (f32[128]{0:T(128)}, f32[128]{0:T(128)S(1)}, u32[]{:S(2)}) copy-start(f32[128]{0:T(128)S(1)} %broadcast_multiply_fusion.5) | copy-start | bytes 1540
  11.1 149.5 %copy-start.34 = (f32[128]{0:T(128)}, f32[128]{0:T(128)S(1)}, u32[]{:S(2)}) copy-start(f32[128]{0:T(128)S(1)} %add_rsqrt_fusion.1) | copy-start | bytes 1540
  166.0 14.5 %all-to-all-start = ((bf16[32,16,192]{2,1,0:T(8,128)(2,1)}), bf16[32,16,192]{2,1,0:T(8,128)(2,1)S(1)}, u32[]{:S(2)}, u32[]{:S(2)}) async-start(bf16[32,16,192]{2,1,0:T(8,128)(2,1)} %bitcast.16), calls=%async_computation | async-start | bytes 524288 | tf_op jit(solution)/shard_map/all_to_all | solution.py:152
  182.9 30.0 %all-to-all-start.1 = ((bf16[32,128,384]{1,2,0:T(8,128)(2,1)}), bf16[32,128,384]{1,2,0:T(8,128)(2,1)}, u32[]{:S(2)}, u32[]{:S(2)}) async-start(bf16[32,128,384]{1,2,0:T(8,128)(2,1)} %bitcast.208), calls=%async_computation.1 | async-start | bytes 6291456 | tf_op jit(solution)/shard_map/all_to_all | solution.py:153
  187.7 172.7 %all-gather.5.cloned.1.call-start = ((), (), s32[]{:S(2)}) async-start(), calls=%async_computation.9 | async-start | bytes 2433024 | tf_op jit(solution)/shard_map/all_gather | solution.py:140
  223.6 33.1 %copy-start.12 = (f32[31,1536]{1,0:T(8,128)S(1)}, f32[31,1536]{1,0:T(8,128)}, u32[]{:S(2)}) copy-start(f32[31,1536]{1,0:T(8,128)} %param.15) | copy-start | bytes 571396
  249.7 110.7 %copy-start = (bf16[1,128,1536]{2,1,0:T(8,128)(2,1)S(1)}, bf16[1,128,1536]{2,1,0:T(8,128)(2,1)}, u32[]{:S(2)}) copy-start(bf16[1,128,1536]{2,1,0:T(8,128)(2,1)} %param.11) | copy-start | bytes 1179652
  251.1 13.7 %all-to-all-start.2 = ((bf16[32,16,192]{2,1,0:T(8,128)(2,1)}), bf16[32,16,192]{2,1,0:T(8,128)(2,1)S(1)}, u32[]{:S(2)}, u32[]{:S(2)}) async-start(bf16[32,16,192]{2,1,0:T(8,128)(2,1)} %reshape_reshape.11), calls=%async_computation.2 | async-start | bytes 524288 | tf_op jit(solution)/shard_map/all_to_all | solution.py:162
  265.2 104.7 %copy-start.7 = (bf16[1,128,1536]{2,1,0:T(8,128)(2,1)S(1)}, bf16[1,128,1536]{2,1,0:T(8,128)(2,1)}, u32[]{:S(2)}) copy-start(bf16[1,128,1536]{2,1,0:T(8,128)(2,1)} %param.17) | copy-start | bytes 1179652
  265.3 104.7 %copy-start.33 = (f32[1536]{0:T(1024)S(1)}, f32[1536]{0:T(1024)}, u32[]{:S(2)}) copy-start(f32[1536]{0:T(1024)} %param.16) | copy-start | bytes 18436
  363.1 2.8 collective-permute-start
  364.4 5.3 collective-permute-start.1
  376.4 2.6 collective-permute-start.2
  377.7 4.8 collective-permute-start.3
  391.1 15.3 %all-to-all-start.3 = ((bf16[32,16,192]{2,1,0:T(8,128)(2,1)}), bf16[32,16,192]{2,1,0:T(8,128)(2,1)S(1)}, u32[]{:S(2)}, u32[]{:S(2)}) async-start(bf16[32,16,192]{2,1,0:T(8,128)(2,1)} %bitcast.34), calls=%async_computation.3 | async-start | bytes 524288 | tf_op jit(solution)/shard_map/all_to_all | solution.py:196
  455.4 12.0 %all-to-all-start.4 = ((bf16[32,16,192]{2,1,0:T(8,128)(2,1)}), bf16[32,16,192]{2,1,0:T(8,128)(2,1)S(1)}, u32[]{:S(2)}, u32[]{:S(2)}) async-start(bf16[32,16,192]{2,1,0:T(8,128)(2,1)} %convert_element_type.132), calls=%async_computation.4 | async-start | bytes 524288 | tf_op jit(solution)/shard_map/all_to_all | solution.py:217
  467.4 30.1 %all-to-all-start.5 = ((bf16[32,128,384]{1,2,0:T(8,128)(2,1)}), bf16[32,128,384]{1,2,0:T(8,128)(2,1)}, u32[]{:S(2)}, u32[]{:S(2)}) async-start(bf16[32,128,384]{1,2,0:T(8,128)(2,1)} %copy.74), calls=%async_computation.5 | async-start | bytes 6291456 | tf_op jit(solution)/shard_map/all_to_all | solution.py:218
  472.7 178.2 %reduce-scatter.5.cloned.1.call-start = ((), (), s32[]{:S(2)}) async-start(), calls=%async_computation.11 | async-start | bytes 2433024 | tf_op jit(solution)/shard_map/reduce_scatter | solution.py:246
  475.0 354.3 %reduce-scatter.3.cloned.1.call-start = ((), (), s32[]{:S(2)}) async-start(), calls=%async_computation.10 | async-start | bytes 7299072 | tf_op jit(solution)/shard_map/reduce_scatter | solution.py:243
  475.7 24.9 %copy-start.9 = (f32[1536]{0:T(1024)S(1)}, f32[1536]{0:T(1024)}, u32[]{:S(2)}) copy-start(f32[1536]{0:T(1024)} %copy-done.8) | copy-start | bytes 18436
  505.9 593.7 %all-reduce.5.cloned.1.call-start = ((), (), s32[]{:S(2)}) async-start(), calls=%async_computation.12 | async-start | bytes 393216 | tf_op jit(solution)/shard_map/psum | solution.py:251
  510.6 662.6 %all-reduce.7.cloned.1.call-start = ((), (), s32[]{:S(2)}) async-start(), calls=%async_computation.13 | async-start | bytes 589824 | tf_op jit(solution)/shard_map/psum | solution.py:253
  (40 other events, 132.8 us)
Sparse Core Ops, SparseCore 0:
  9.8 150.7 all-gather.2
  190.4 170.0 all-gather.4
  476.1 174.8 reduce-scatter.4
  653.3 175.8 reduce-scatter.2
  835.2 264.4 all-reduce.4
  1102.2 71.0 all-reduce.6
where the time goes:
time: 1190 us
  waiting for transfers between devices  874 us (73%)
  blocking collectives  108 us (9%)
  matrix products  75.5 us (6%)
  local copies, waits for them, and re-layouts  47.7 us (4%)
  starting transfers between devices  39.2 us (3%)
  other arithmetic  25.7 us (2%)
  between operations  15.4 us (1%)
    psum x1, waiting for transfers between devices, local(): lax.psum((norms_local, kernel_grad, bias_grad), ('dp', 'seq'))  269 us
    reduce_scatter x1, waiting for transfers between devices, local(): lax.psum_scatter(proj_whole.astype(jnp.bfloat16), 'seq', scatter_dimensio...  178 us
    all_gather x1, waiting for transfers between devices, local(): lax.all_gather(w_qkv, 'seq', axis=0, tiled=True)  149 us
    psum x1, blocking collectives, local(): lax.psum((norms_local, kernel_grad, bias_grad), ('dp', 'seq'))  108 us
    all_gather x1, waiting for transfers between devices, local(): lax.all_gather(w_out, 'seq', axis=0, tiled=True)  95.2 us
    psum x1, waiting for transfers between devices, local(): lax.psum(proj_sum.astype(jnp.bfloat16), 'dp').astype(jnp.float32)  73.6 us
    reduce_scatter x1, waiting for transfers between devices, local(): lax.psum_scatter(out_whole.astype(jnp.bfloat16), 'seq', scatter_dimension...  27 us
    all_to_all x1, waiting for transfers between devices, local(): lax.all_to_all(key_send, 'seq', split_axis=0, concat_axis=0, tiled=True)  24.2 us
  transfers between devices with their start and end apart: 16, of which 14 were waited for; matrix products, arithmetic and copies ran while one was open for 6% of the time, Pallas kernels for 0%

commit v1 on v0

v1 whole, which is shorter than its diff:
```python
import functools

import jax
import jax.numpy as jnp
from jax import lax
from jax.experimental import pallas as pl
from jax.experimental.pallas import tpu as pltpu
from jax.sharding import PartitionSpec as P

EPS = 1e-05
GROUPS = 4
PLANE = 8
HEADS = 3
HD = 64
F32 = jnp.float32
BF16 = jnp.bfloat16


def group_of(kind):
    seq, dp = lax.axis_index("seq"), lax.axis_index("dp")
    if kind == "y":
        return 4, seq // 8, lambda i: {"seq": i * 8 + seq % 8}
    if kind == "plane":
        return 8, seq % 8, lambda i: {"seq": (seq // 8) * 8 + i}
    if kind == "seq":
        return 32, seq, lambda i: {"seq": i}
    return 8, dp, lambda i: {"dp": i}


SIZES = {"y": 4, "plane": 8, "seq": 32, "dp": 8}


def greet(kinds):
    if "seq" in kinds:
        kinds = [k for k in kinds if k not in ("y", "plane")]
    barrier = pltpu.get_barrier_semaphore()
    total = 0
    for kind in kinds:
        count, me, where = group_of(kind)
        for k in range(1, count):
            pl.semaphore_signal(barrier, inc=1, device_id=where((me + k) % count))
        total += count - 1
    pl.semaphore_wait(barrier, total)


def exchange_kernel(jobs, *refs):
    n = len(jobs)
    ins, outs, sems = refs[:n], refs[n : 2 * n], refs[2 * n :]
    greet(sorted({kind for kind, _ in jobs}))
    copies = []
    for j, (kind, mode) in enumerate(jobs):
        count, me, where = group_of(kind)
        send, recv, own = sems[3 * j : 3 * j + 3]
        for k in range(1, count):
            peer = (me + k) % count
            src = ins[j] if mode == "gather" else ins[j].at[peer]
            copy = pltpu.make_async_remote_copy(
                src_ref=src,
                dst_ref=outs[j].at[me],
                send_sem=send.at[k - 1],
                recv_sem=recv.at[k - 1],
                device_id=where(peer),
            )
            copy.start()
            copies.append(copy)
        src = ins[j] if mode == "gather" else ins[j].at[me]
        mine = pltpu.make_async_copy(src, outs[j].at[me], own.at[0])
        mine.start()
        copies.append(mine)
    for copy in copies:
        copy.wait()


def exchange(cid, *jobs):
    arrays = [job[0] for job in jobs]
    kinds = [(job[1], job[2]) for job in jobs]
    shapes, scratch = [], []
    for array, kind, mode in jobs:
        count = SIZES[kind]
        shape = (count, *array.shape) if mode == "gather" else array.shape
        shapes.append(jax.ShapeDtypeStruct(shape, array.dtype))
        scratch += [
            pltpu.SemaphoreType.DMA((count - 1,)),
            pltpu.SemaphoreType.DMA((count - 1,)),
            pltpu.SemaphoreType.DMA((1,)),
        ]
    return pl.pallas_call(
        functools.partial(exchange_kernel, kinds),
        out_shape=shapes,
        in_specs=[pl.BlockSpec(memory_space=pl.ANY)] * len(jobs),
        out_specs=[pl.BlockSpec(memory_space=pl.ANY)] * len(jobs),
        scratch_shapes=scratch,
        compiler_params=pltpu.CompilerParams(collective_id=cid, has_side_effects=True),
        name=f"exchange{cid}",
    )(*arrays)


def halo(array, width):
    devices, length = lax.axis_size("seq"), array.shape[0]
    up = [(i, i + 1) for i in range(devices - 1)]
    down = [(j, i) for i, j in up]
    before = lax.ppermute(array[length - width :], "seq", up)
    after = lax.ppermute(array[:width], "seq", down)
    return jnp.concatenate([before, array, after], axis=0)


def layer_norm(values, gain):
    center = values - jnp.mean(values, axis=-1, keepdims=True)
    spread = jnp.mean(center * center, axis=-1, keepdims=True)
    inverse = lax.rsqrt(spread + EPS)
    normed = center * inverse
    return (normed * gain, normed, inverse)


def norm_back(grad, normed, inverse, gain):
    scaled = grad * gain
    inner = (
        scaled
        - jnp.mean(scaled, axis=-1, keepdims=True)
        - normed * jnp.mean(scaled * normed, axis=-1, keepdims=True)
    )
    return (inverse * inner, jnp.sum(grad * normed, axis=0))


def head_forward(query, keys, values):
    factor = query.shape[-1] ** (-0.5)
    scores = (
        lax.dot_general(query, keys, (((1,), (1,)), ((), ())), preferred_element_type=F32) * factor
    )
    top = jnp.max(scores, axis=-1, keepdims=True)
    expo = jnp.exp(scores - top)
    total = jnp.sum(expo, axis=-1, keepdims=True)
    probs = (expo / total).astype(BF16)
    attended = jnp.dot(probs, values, preferred_element_type=F32).astype(BF16)
    return (attended, top[:, 0] + jnp.log(total[:, 0]))


def head_backward(query, keys, values, attended, log_total, grad_attended):
    factor = query.shape[-1] ** (-0.5)
    scores = (
        lax.dot_general(query, keys, (((1,), (1,)), ((), ())), preferred_element_type=F32) * factor
    )
    probs = jnp.exp(scores - log_total[:, None])
    value_grads = lax.dot_general(
        probs.astype(BF16), grad_attended, (((0,), (0,)), ((), ())), preferred_element_type=F32
    )
    prob_grads = lax.dot_general(
        grad_attended, values, (((1,), (1,)), ((), ())), preferred_element_type=F32
    )
    delta = jnp.sum(
        grad_attended.astype(F32) * attended.astype(F32), axis=-1, keepdims=True
    )
    score_grads = (probs * (prob_grads - delta) * factor).astype(BF16)
    query_grads = jnp.dot(score_grads, keys, preferred_element_type=F32)
    key_grads = lax.dot_general(
        score_grads, query, (((0,), (0,)), ((), ())), preferred_element_type=F32
    )
    return (query_grads, key_grads, value_grads)


def depthwise(wide, kernel, length):
    total = jnp.zeros((length, wide.shape[1]), F32)
    for tap in range(kernel.shape[0]):
        total = total + wide[tap : tap + length] * kernel[tap]
    return total


def split_heads(block):
    return block.reshape(block.shape[0], HEADS, -1).transpose(1, 0, 2)


def join_heads(block):
    return block.transpose(1, 0, 2).reshape(block.shape[1], -1)


def matmul(a, b, dims=((1,), (0,))):
    return lax.dot_general(a, b, (dims, ((), ())), preferred_element_type=F32)


def local(frames, w_qkv, w_out, norm_gains, conv_kernel, conv_bias, out_grad):
    inputs = frames[0].astype(F32)
    rows, model = inputs.shape
    shard, three = w_qkv.shape
    width = three // (3 * GROUPS)
    trio = 3 * width
    share_out = w_out.shape[0]
    many = GROUPS * rows

    shifted, normed1, inverse1 = layer_norm(inputs, norm_gains[0])
    hidden = shifted.astype(BF16)
    w_parts = (
        w_qkv.reshape(shard, 3, GROUPS, width).transpose(2, 0, 1, 3).reshape(GROUPS, shard, trio)
    )
    hidden_all, w_mine = exchange(0, (hidden, "y", "gather"), (w_parts, "y", "a2a"))
    w_all, out_all = exchange(1, (w_mine, "plane", "gather"), (w_out, "plane", "gather"))
    hidden_all = hidden_all.reshape(many, model)
    w_group = w_all.transpose(1, 0, 2, 3).reshape(model, trio)
    out_group = out_all.reshape(width, model)

    projected = matmul(hidden_all, w_group).astype(BF16)
    (pairs,) = exchange(2, (projected[:, width:], "plane", "gather"))
    pairs = pairs.reshape(PLANE * many, 2 * width)
    query_heads = split_heads(projected[:, :width])
    key_heads = split_heads(pairs[:, :width])
    value_heads = split_heads(pairs[:, width:])
    attended_heads, log_total = lax.map(
        lambda item: head_forward(*item), (query_heads, key_heads, value_heads)
    )
    attended = join_heads(attended_heads)
    out_parts = matmul(attended, out_group).astype(BF16).reshape(GROUPS, rows, model)
    (out_terms,) = exchange(3, (out_parts, "y", "a2a"))
    mixed = (inputs + jnp.sum(out_terms.astype(F32), axis=0)).astype(BF16)

    mixed32 = mixed.astype(F32)
    shifted2, normed2, inverse2 = layer_norm(mixed32, norm_gains[1])
    conv_in = shifted2.astype(BF16)
    taps = conv_kernel.shape[0]
    half = (taps - 1) // 2
    conv_wide = halo(conv_in, half).astype(F32)
    preact = depthwise(conv_wide, conv_kernel, rows) + conv_bias
    sigma = jax.nn.sigmoid(preact)
    output = (mixed32 + preact * sigma).astype(BF16)
    upstream = out_grad[0].astype(F32)
    grad_pre = (upstream * sigma * (1.0 + preact * (1.0 - sigma))).astype(BF16)
    grad_pre_wide = halo(grad_pre, half).astype(F32)
    grad_conv = depthwise(grad_pre_wide, conv_kernel[::-1], rows)
    grad_pre_float = grad_pre.astype(F32)
    kernel_grad = jnp.stack(
        [jnp.sum(grad_pre_float * conv_wide[tap : tap + rows], axis=0) for tap in range(taps)]
    )
    bias_grad = jnp.sum(grad_pre_float, axis=0)
    mixed_norm_grad, gain2_grad = norm_back(grad_conv, normed2, inverse2, norm_gains[1])
    grad_mixed = (upstream + mixed_norm_grad).astype(BF16)

    (mixed_all,) = exchange(4, (grad_mixed, "y", "gather"))
    mixed_all = mixed_all.reshape(many, model)
    grad_attended = matmul(mixed_all, out_group, ((1,), (1,))).astype(BF16)
    query_grads, key_grads, value_grads = lax.map(
        lambda item: head_backward(*item),
        (
            query_heads,
            key_heads,
            value_heads,
            attended_heads,
            log_total,
            split_heads(grad_attended),
        ),
    )
    pair_parts = (
        jnp.concatenate([join_heads(key_grads), join_heads(value_grads)], axis=1)
        .reshape(PLANE, many, 2 * width)
        .astype(BF16)
    )
    (pair_terms,) = exchange(5, (pair_parts, "plane", "a2a"))
    pair_grads = jnp.sum(pair_terms.astype(F32), axis=0).astype(BF16)
    grad_proj = jnp.concatenate([join_heads(query_grads).astype(BF16), pair_grads], axis=1)

    hid_parts = matmul(grad_proj, w_group, ((1,), (1,))).astype(BF16).reshape(GROUPS, rows, model)
    w_grad = (
        matmul(hidden_all, grad_proj, ((0,), (0,)))
        .astype(BF16)
        .reshape(GROUPS, PLANE, shard, trio)
        .transpose(1, 0, 2, 3)
    )
    out_grad_parts = (
        matmul(attended, mixed_all, ((0,), (0,))).astype(BF16).reshape(PLANE, share_out, model)
    )
    hid_terms, w_terms, out_grad_terms = exchange(
        6, (hid_parts, "y", "a2a"), (w_grad, "plane", "a2a"), (out_grad_parts, "plane", "a2a")
    )
    grad_hidden = jnp.sum(hid_terms.astype(F32), axis=0)
    input_norm_grad, gain1_grad = norm_back(grad_hidden, normed1, inverse1, norm_gains[0])
    grad_input = (grad_mixed.astype(F32) + input_norm_grad).astype(BF16)

    dp = lax.axis_size("dp")
    w_sum = jnp.sum(w_terms.astype(F32), axis=0).astype(BF16)
    out_sum = jnp.sum(out_grad_terms.astype(F32), axis=0).astype(BF16)
    lanes = 128
    w_split = w_sum.reshape(GROUPS, dp, -1, lanes).transpose(1, 0, 2, 3)
    out_split = out_sum.reshape(dp, -1, lanes)
    small = jnp.concatenate([gain1_grad[None], gain2_grad[None], kernel_grad, bias_grad[None]])
    count = small.shape[0]
    small_split = small.reshape(count, dp, -1).transpose(1, 0, 2)
    w_dp, out_dp, small_dp = exchange(
        7, (w_split, "dp", "a2a"), (out_split, "dp", "a2a"), (small_split, "dp", "a2a")
    )
    w_share = jnp.sum(w_dp.astype(F32), axis=0).astype(BF16)
    out_share = jnp.sum(out_dp.astype(F32), axis=0).astype(BF16)
    small_share = jnp.sum(small_dp, axis=0)
    w_home, small_seq = exchange(8, (w_share, "y", "a2a"), (small_share, "seq", "gather"))
    small_sum = jnp.sum(small_seq, axis=0)
    w_fin, out_fin, small_fin = exchange(
        9, (w_home, "dp", "gather"), (out_share, "dp", "gather"), (small_sum, "dp", "gather")
    )
    grad_qkv = (
        w_fin.transpose(1, 0, 2, 3)
        .reshape(GROUPS, shard, 3, width)
        .transpose(1, 2, 0, 3)
        .reshape(shard, three)
    )
    grad_out = out_fin.reshape(share_out, model)
    small_all = small_fin.transpose(1, 0, 2).reshape(count, model)
    return (
        output[None],
        grad_input[None],
        grad_qkv,
        grad_out,
        small_all[:2],
        small_all[2 : count - 1],
        small_all[count - 1],
    )


def solution(mesh):
    in_specs = (
        P("dp", "seq", None),
        P("seq", None),
        P("seq", None),
        P(),
        P(),
        P(),
        P("dp", "seq", None),
    )
    out_specs = (
        P("dp", "seq", None),
        P("dp", "seq", None),
        P("seq", None),
        P("seq", None),
        P(),
        P(),
        P(),
    )
    return jax.shard_map(local, mesh=mesh, in_specs=in_specs, out_specs=out_specs, check_vma=False)
```

time: 1190 us -> 577 us (0.48)
  waiting for transfers between devices: 874 us -> 2.16 us
  Pallas kernels: 0 us -> 305 us
  blocking collectives: 108 us -> 0 us
  local copies, waits for them, and re-layouts: 47.7 us -> 132 us
  other arithmetic: 25.7 us -> 55.8 us
  starting transfers between devices: 39.2 us -> 12.5 us
  matrix products: 75.5 us -> 60.6 us
  between operations: 15.4 us -> 1.71 us
    psum x2 -> x0, waiting for transfers between devices: 343 us -> none  [the longest x1 269 us: local(): lax.psum((norms_local, kernel_grad, bias_grad), ('dp', 'seq'))]
    pallas_call x0 -> x10, Pallas kernels: none -> 305 us  [exchange(): pl.pallas_call(functools.partial(exchange_kernel, kinds), out_shape=shape...]
    all_gather x2 -> x0, waiting for transfers between devices: 245 us -> none  [the longest x1 149 us: local(): lax.all_gather(w_qkv, 'seq', axis=0, tiled=True)]
    reduce_scatter x2 -> x0, waiting for transfers between devices: 205 us -> none  [the longest x1 178 us: local(): lax.psum_scatter(proj_whole.astype(jnp.bfloat16), 'seq', scatter_dimensio...]
    psum x1 -> x0, blocking collectives: 108 us -> none  [local(): lax.psum((norms_local, kernel_grad, bias_grad), ('dp', 'seq'))]
    all_to_all x6 -> x0, waiting for transfers between devices: 71.9 us -> none  [the longest x1 24.2 us: local(): lax.all_to_all(key_send, 'seq', split_axis=0, concat_axis=0, tiled=True)]
    concatenate x0 -> x35, local copies, waits for them, and re-layouts: none -> 51.8 us  [local(): jnp.concatenate([gain1_grad[None], gain2_grad[None], kernel_grad, bias_gr...]
    all_to_all x6 -> x0, starting transfers between devices: 33.6 us -> none  [the longest x1 7.34 us: local(): lax.all_to_all(to_groups(grad_attended, count, groups, quarters), 'seq',...]
  transfers between devices with their start and end apart: 16 -> 4, of which waited for: 14 -> 1; matrix products, arithmetic and copies ran while one was open for 6% -> 8% of each run, Pallas kernels for 0% -> 0%
where the time goes in v1:
time: 577 us; the launch traced here: 569 us
  Pallas kernels  305 us (53%)
  local copies, waits for them, and re-layouts  132 us (23%)
  matrix products  60.6 us (11%)
  other arithmetic  55.8 us (10%)
  starting transfers between devices  12.5 us (2%)
    pallas_call x10, Pallas kernels, exchange(): pl.pallas_call(functools.partial(exchange_kernel, kinds), out_shape=shape...  305 us
    concatenate x35, local copies, waits for them, and re-layouts, local(): jnp.concatenate([gain1_grad[None], gain2_grad[None], kernel_grad, bias_gr...  51.8 us
    dot_general x6, matrix products, matmul(): return lax.dot_general(a, b, (dims, ((), ())), preferred_element_type=F32)  15.1 us
    unnamed x94, local copies, waits for them, and re-layouts  14.9 us
    dot_general x3, matrix products, head_backward(): lax.dot_general(grad_attended, values, (((1,), (1,)), ((), ())), preferre...  14 us
    dot_general x3, matrix products, head_forward(): attended = jnp.dot(probs, values, preferred_element_type=F32).astype(BF16)  11.8 us
  transfers between devices with their start and end apart: 4, of which 1 were waited for; matrix products, arithmetic and copies ran while one was open for 8% of the time, Pallas kernels for 0%

profile of v1, /device:TPU:1, one launch (start us, length us, event | category | flops | bytes accessed | tf_op | source)
XLA Modules:
  0.0 569.1 jit_solution(15815826590177924589)
XLA Ops:
  8.3 24.3 %exchange0.1 = (bf16[4,128,1536]{2,1,0:T(8,128)(2,1)}, bf16[4,48,576]{2,1,0:T(8,128)(2,1)}) custom-call(bf16[128,1536]{1,0:T(8,128)(2,1)} %fusion.64.refs_0_, bf16[4,48,576]{2,1,0:T(8,128)(2,1)} %reshape.230.refs_1_), custom_call_target="tpu_custom_call" | custom-call | tf_op jit(solution)/shard_map/exchange0/pallas_call | solution.py:87
  32.6 36.2 %exchange1.1 = (bf16[8,4,48,576]{3,2,1,0:T(8,128)(2,1)}, bf16[8,24,1536]{2,1,0:T(8,128)(2,1)}) custom-call(bf16[4,48,576]{2,1,0:T(8,128)(2,1)} %get-tuple-element.110.refs_0_, bf16[24,1536]{1,0:T(8,128)(2,1)} %refs_1_.1), custom_call_target="tpu_custom_call" | custom-call | tf_op jit(solution)/shard_map/exchange1/pallas_call | solution.py:87
  73.3 38.1 %exchange2.1 = bf16[8,512,384]{2,1,0:T(8,128)(2,1)} custom-call(bf16[512,384]{1,0:T(8,128)(2,1)} %slice.529.refs_0_), custom_call_target="tpu_custom_call" | custom-call | tf_op jit(solution)/shard_map/exchange2/pallas_call | solution.py:87
  111.4 4.7 fusion.145
  116.1 4.3 copy.72
  120.4 4.1 copy.53
  130.3 24.3 %while.26 = (s32[]{:T(128)}, bf16[3,512,64]{1,2,0:T(8,128)(2,1)}, f32[3,512]{1,0:T(4,128)}, bf16[3,512,64]{2,1,0:T(8,128)(2,1)S(1)}, bf16[3,4096,64]{2,1,0:T(8,1...) while((s32[]{:T(128)}, bf16[3,512,64]{1,2,0:T(8,128)(2,1)}, f32[3,512]{1,0:T(4,128)}, ...), condition=%wide.region_5.6_spmd, body=%wide.region_2.5_spmd.sunk | while | flops 555777536 | bytes 27482208 | solution.py:206
  157.6 25.0 %exchange3.1 = bf16[4,128,1536]{2,1,0:T(8,128)(2,1)} custom-call(bf16[4,128,1536]{2,1,0:T(8,128)(2,1)} %bitcast.213), custom_call_target="tpu_custom_call" | custom-call | tf_op jit(solution)/shard_map/exchange3/pallas_call | solution.py:87
  187.9 5.8 %collective-permute-start = (bf16[15,1536]{1,0:T(8,128)(2,1)}, bf16[15,1536]{1,0:T(8,128)(2,1)}, u32[]{:S(2)}, u32[]{:S(2)}) collective-permute-start(bf16[15,1536]{1,0:T(8,128)(2,1)} %get-tuple-element.287), channel_id=1, source_target_pairs={{0,1},{1,2},{2,3},{3,4},{4,5},{5,6},{6,7},{7,8},{8,9},{9,10},{10,1... | collective-permute-start | bytes 138248 | tf_op jit(solution)/shard_map/ppermute | solution.py:102
  200.0 8.4 %fusion.107 = (f32[1536]{0:T(1024)}, f32[1536]{0:T(1024)}, f32[1536]{0:T(1024)}, f32[1536]{0:T(1024)}, f32[1536]{0:T(1024)}, /*index=5*/f32[1536]{0:T(1024)}, f3...) fusion(f32[158,1536]{1,0:T(8,128)S(1)} %maximum_convert_fusion,, ...), kind=kLoop, calls=%fused_computation.167 | loop fusion | flops 21402624 | bytes 26259456 | tf_op jit(solution)/shard_map/reduce_sum | solution.py:229
  261.4 6.8 %fusion.62 = (f32[1536]{0:T(1024)}, f32[128]{0:T(128)S(1)}, f32[128]{0:T(128)S(1)}, f32[128,1536]{1,0:T(8,128)S(1)}) fusion(bf16[128,1536]{1,0:T(8,128)(2,1)} %copy-done.2, f32[128]{0:T(128)S(1)} %add_rsqrt_fusion, f32[128]{0:T(128)S(1)} %broadcast_multiply_fusion.4, f32[1536]{0:T(1024)S(1)} %get-tuple-element.240, f32[1536]{0:T(1024)} %get-tuple-element.209, ...), kind=kLoop, calls=%fused_computation.122 | loop fusion | flops 13760768 | bytes 25763840 | tf_op jit(solution)/shard_map/reduce_sum | solution.py:122
  269.7 26.5 %exchange4.1 = bf16[4,128,1536]{2,1,0:T(8,128)(2,1)} custom-call(bf16[128,1536]{1,0:T(8,128)(2,1)} %get-tuple-element.283.refs_0_), custom_call_target="tpu_custom_call" | custom-call | tf_op jit(solution)/shard_map/exchange4/pallas_call | solution.py:87
  303.8 48.9 %while.27 = (s32[]{:T(128)}, bf16[3,512,64]{1,2,0:T(8,128)(2,1)}, bf16[3,4096,64]{1,2,0:T(8,128)(2,1)}, bf16[3,4096,64]{1,2,0:T(8,128)(2,1)}, bf16[3,512,64]{2,1...) while((s32[]{:T(128)}, bf16[3,512,64]{1,2,0:T(8,128)(2,1)}, ...), condition=%wide.region_13.14_spmd, body=%wide.region_11.13_spmd.sunk | while | flops 1361182208 | bytes 71583048 | solution.py:238
  311.9 4.7 multiply_convert_fusion.2
  328.2 4.7 multiply_convert_fusion.2
  344.5 4.7 multiply_convert_fusion.2
  362.1 4.3 copy.59
  366.4 4.4 pad_maximum_fusion.refs_0_
  370.8 37.0 %exchange5.1 = bf16[8,512,384]{2,1,0:T(8,128)(2,1)} custom-call(bf16[8,512,384]{2,1,0:T(8,128)(2,1)} %pad_maximum_fusion.refs_0_), custom_call_target="tpu_custom_call" | custom-call | tf_op jit(solution)/shard_map/exchange5/pallas_call | solution.py:87
  420.5 42.5 %exchange6.1 = (bf16[4,128,1536]{2,1,0:T(8,128)(2,1)}, bf16[8,4,48,576]{3,2,1,0:T(8,128)(2,1)}, bf16[8,24,1536]{2,1,0:T(8,128)(2,1)}) custom-call(bf16[4,128,1536]{2,1,0:T(8,128)(2,1)} %bitcast.226, bf16[8,4,48,576]{3,2,1,0:T(8,128)(2,1)} %bitcast.208, bf16[8,24,1536]{2,1,0:T(8,128)(2,1)} %bitcast.218), custom_call_target="tpu_custom_call" | custom-call | tf_op jit(solution)/shard_map/exchange6/pallas_call | solution.py:87
  470.1 6.6 %concatenate.130 = f32[34,8,192]{2,0,1:T(8,128)} concatenate(f32[1,8,192]{2,0,1:T(1,128)} %concatenate.96, f32[1,8,192]{2,0,1:T(1,128)} %concatenate.97, f32[1,8,192]{2,0,1:T(1,128)} %concatenate.98, f32[1,8,192]{2,0,1:T(1,128)S(1)} %copy-done.24, f32[1,8,192]{2,0,1:T(1,128)S(1)} %copy-done.25, f32[1,8,192]{2,0,1:T(1,128)S(1)} %copy-done.26, f32[1,8,192]{2,0,1:T(1,128)S(1)} %copy-done.27, ...), dimensions={0} | concatenate | bytes 417792 | tf_op jit(solution)/shard_map/concatenate | solution.py:281
  476.7 25.6 %exchange7.1 = (bf16[8,4,27,128]{3,2,1,0:T(8,128)(2,1)}, bf16[8,36,128]{2,1,0:T(8,128)(2,1)}, f32[8,34,192]{2,1,0:T(8,128)}) custom-call(bf16[8,4,27,128]{3,2,1,0:T(8,128)(2,1)} %bitcast.228, bf16[8,36,128]{2,1,0:T(8,128)(2,1)} %reshape.246.refs_1_, f32[8,34,192]{2,1,0:T(8,128)} %bitcast.227), custom_call_target="tpu_custom_call" | custom-call | tf_op jit(solution)/shard_map/exchange7/pallas_call | solution.py:87
  507.1 27.6 %exchange8.1 = (bf16[4,27,128]{2,1,0:T(8,128)(2,1)}, f32[32,34,192]{2,1,0:T(8,128)}) custom-call(bf16[4,27,128]{2,1,0:T(8,128)(2,1)} %reduce_sum.539.refs_0_, f32[34,192]{1,0:T(8,128)} %reduce_sum.540.refs_1_), custom_call_target="tpu_custom_call" | custom-call | tf_op jit(solution)/shard_map/exchange8/pallas_call | solution.py:87
  536.8 21.7 %exchange9.1 = (bf16[8,4,27,128]{3,2,1,0:T(8,128)(2,1)}, bf16[8,36,128]{2,1,0:T(8,128)(2,1)}, f32[8,34,192]{2,1,0:T(8,128)}) custom-call(bf16[4,27,128]{2,1,0:T(8,128)(2,1)} %get-tuple-element.123.refs_0_, bf16[36,128]{1,0:T(8,128)(2,1)} %reduce_sum.541.refs_1_, f32[34,192]{1,0:T(8,128)} %reduce_sum.542.refs_2_), custom_call_target="tpu_custom_call" | custom-call | tf_op jit(solution)/shard_map/exchange9/pallas_call | solution.py:87
  (289 shorter events, 199.1 us)
Async XLA Ops:
  1.8 68.7 %copy-start.42 = (f32[128]{0:T(128)}, f32[128]{0:T(128)S(1)}, u32[]{:S(2)}) copy-start(f32[128]{0:T(128)S(1)} %broadcast_multiply_fusion.5) | copy-start | bytes 1540
  3.1 67.5 %copy-start.45 = (f32[128]{0:T(128)}, f32[128]{0:T(128)S(1)}, u32[]{:S(2)}) copy-start(f32[128]{0:T(128)S(1)} %add_rsqrt_fusion.1) | copy-start | bytes 1540
  3.9 66.7 %copy-start.20 = (f32[1536]{0:T(1024)}, f32[1536]{0:T(1024)S(1)}, u32[]{:S(2)}) copy-start(f32[1536]{0:T(1024)S(1)} %get-tuple-element.241) | copy-start | bytes 18436
  32.6 38.0 %copy-start.50 = (bf16[4,128,1536]{2,1,0:T(8,128)(2,1)S(1)}, bf16[4,128,1536]{2,1,0:T(8,128)(2,1)}, u32[]{:S(2)}) copy-start(bf16[4,128,1536]{2,1,0:T(8,128)(2,1)} %get-tuple-element.109) | copy-start | bytes 4718596
  182.5 12.5 %copy-start.19 = (f32[31,1536]{1,0:T(8,128)S(1)}, f32[31,1536]{1,0:T(8,128)}, u32[]{:S(2)}) copy-start(f32[31,1536]{1,0:T(8,128)} %param.15) | copy-start | bytes 571396
  187.9 8.8 %collective-permute-start = (bf16[15,1536]{1,0:T(8,128)(2,1)}, bf16[15,1536]{1,0:T(8,128)(2,1)}, u32[]{:S(2)}, u32[]{:S(2)}) collective-permute-start(bf16[15,1536]{1,0:T(8,128)(2,1)} %get-tuple-element.287), channel_id=1, source_target_pairs={{0,1},{1,2},{2,3},{3,4},{4,5},{5,6},{6,7},{7,8},{8,9},{9,10},{10,1... | collective-permute-start | bytes 138248 | tf_op jit(solution)/shard_map/ppermute | solution.py:102
  193.7 5.1 collective-permute-start.1
  208.4 7.9 %copy-start.4 = (bf16[128,1536]{1,0:T(8,128)(2,1)}, bf16[128,1536]{1,0:T(8,128)(2,1)S(1)}, u32[]{:S(2)}) copy-start(bf16[128,1536]{1,0:T(8,128)(2,1)S(1)} %get-tuple-element.274) | copy-start | bytes 1179652
  209.1 51.1 %collective-permute-start.2 = (bf16[15,1536]{1,0:T(8,128)(2,1)}, bf16[15,1536]{1,0:T(8,128)(2,1)}, u32[]{:S(2)}, u32[]{:S(2)}) collective-permute-start(bf16[15,1536]{1,0:T(8,128)(2,1)} %get-tuple-element.285), channel_id=1, source_target_pairs={{0,1},{1,2},{2,3},{3,4},{4,5},{5,6},{6,7},{7,8},{8,9},{9,10},{10,1... | collective-permute-start | bytes 138248 | tf_op jit(solution)/shard_map/ppermute | solution.py:102
  213.2 47.0 %collective-permute-start.3 = (bf16[15,1536]{1,0:T(8,128)(2,1)}, bf16[15,1536]{1,0:T(8,128)(2,1)}, u32[]{:S(2)}, u32[]{:S(2)}) collective-permute-start(bf16[15,1536]{1,0:T(8,128)(2,1)} %get-tuple-element.286), channel_id=1, source_target_pairs={{1,0},{2,1},{3,2},{4,3},{5,4},{6,5},{7,6},{8,7},{9,8},{10,9},{11,1... | collective-permute-start | bytes 138248 | tf_op jit(solution)/shard_map/ppermute | solution.py:103
  261.4 6.9 %copy-start.3 = (bf16[128,1536]{1,0:T(8,128)(2,1)S(1)}, bf16[128,1536]{1,0:T(8,128)(2,1)}, u32[]{:S(2)}) copy-start(bf16[128,1536]{1,0:T(8,128)(2,1)} %copy-done.2) | copy-start | bytes 1179652
  261.4 6.8 %copy-start.6 = (f32[128,1536]{1,0:T(8,128)S(1)}, f32[128,1536]{1,0:T(8,128)}, u32[]{:S(2)}) copy-start(f32[128,1536]{1,0:T(8,128)} %get-tuple-element.275) | copy-start | bytes 2359300
  261.4 6.8 %copy-start.15 = (bf16[1,128,1536]{2,1,0:T(8,128)(2,1)S(1)}, bf16[1,128,1536]{2,1,0:T(8,128)(2,1)}, u32[]{:S(2)}) copy-start(bf16[1,128,1536]{2,1,0:T(8,128)(2,1)} %param.17) | copy-start | bytes 1179652
  420.5 44.4 %copy-start = (bf16[1,128,1536]{2,1,0:T(8,128)(2,1)S(1)}, bf16[1,128,1536]{2,1,0:T(8,128)(2,1)}, u32[]{:S(2)}) copy-start(bf16[1,128,1536]{2,1,0:T(8,128)(2,1)} %param.11) | copy-start | bytes 1179652
  420.5 44.4 %copy-start.21 = (f32[1536]{0:T(1024)S(1)}, f32[1536]{0:T(1024)}, u32[]{:S(2)}) copy-start(f32[1536]{0:T(1024)} %copy-done.20) | copy-start | bytes 18436
  420.5 44.4 %copy-start.43 = (f32[128]{0:T(128)S(1)}, f32[128]{0:T(128)}, u32[]{:S(2)}) copy-start(f32[128]{0:T(128)} %copy-done.42) | copy-start | bytes 1540
  420.5 44.4 %copy-start.46 = (f32[128]{0:T(128)S(1)}, f32[128]{0:T(128)}, u32[]{:S(2)}) copy-start(f32[128]{0:T(128)} %copy-done.45) | copy-start | bytes 1540
  463.1 5.5 copy-start.8
  465.0 5.0 copy-start.22
  468.9 92.3 %copy-start.49 = (f32[128]{0:T(128)S(1)}, f32[128]{0:T(128)}, u32[]{:S(2)}) copy-start(f32[128]{0:T(128)} %get-tuple-element.205) | copy-start | bytes 1540
  468.9 92.3 %copy-start.48 = (f32[128]{0:T(128)S(1)}, f32[128]{0:T(128)}, u32[]{:S(2)}) copy-start(f32[128]{0:T(128)} %get-tuple-element.206) | copy-start | bytes 1540
  503.9 63.8 %copy-start.5 = (bf16[128,1536]{1,0:T(8,128)(2,1)S(1)}, bf16[128,1536]{1,0:T(8,128)(2,1)}, u32[]{:S(2)}) copy-start(bf16[128,1536]{1,0:T(8,128)(2,1)} %get-tuple-element.283.refs_0_) | copy-start | bytes 1179652
  503.9 63.8 %copy-start.44 = (f32[128]{0:T(128)S(1)}, f32[128]{0:T(128)}, u32[]{:S(2)}) copy-start(f32[128]{0:T(128)} %copy-done.42) | copy-start | bytes 1540
  503.9 63.8 %copy-start.47 = (f32[128]{0:T(128)S(1)}, f32[128]{0:T(128)}, u32[]{:S(2)}) copy-start(f32[128]{0:T(128)} %copy-done.45) | copy-start | bytes 1540
  (46 other events, 150.8 us)
